TPU v7x, 32 devices: a whole 2x2x4 slice. The times are simulated.
32 devices in a mesh: grp: 2 (over y), ta: 16 (over z, x, core).
Axes of the slice: x: 2, y: 2, z: 4, core: 2. Of those that a mesh axis runs over, the one named last changes fastest.
Arguments:
- perambulator: bfloat16 [2, 16, 768, 2, 512], P('grp', None, 'ta'), parts along dimension 0, may hold values from -1.1953125 to 1.1953125
- batch_columns: int32 [32], P(('grp', 'ta')), parts along dimension 0, may hold values from 1 to 48, 512 in all
- sink_operator: int32 [2, 16], replicated, may hold values from 0 to 1
- sink_elemental: bfloat16 [8, 16, 2, 128, 128], P('grp'), parts along dimension 0, may hold values from -0.375 to 0.375
- source_elemental: bfloat16 [2, 2, 128, 128], P('grp'), parts along dimension 0, may hold values from -0.375 to 0.375
Outputs:
- loops: bfloat16 [32, 2, 512, 512], P(('grp', 'ta')), parts along dimension 0
There are 2 independent parts, one for each index of `grp`. A program takes and returns all parts, laid end to end along the dimension named above; an argument that names none is the same for every part. Nothing has to cross between parts.
Inputs may be any that keep to these rules, and one draw needn't show every extreme that they name: Batch d holds columns starts[d] to starts[d] + batch_columns[d] - 1 of every source and sink time, in order, in its first batch_columns[d] slots; later slots hold nothing that is read. The entries sum to 512 and the largest equals 48.
All inputs are finite; a program needn't handle non-finite values. No bound on the sum of `batch_columns` on one device may be relied on, other than what follows from the above.
Results may differ from a plain program's by a relative error of at most 0.0057.
Values may be sent and summed in bfloat16 or wider, within the bound.
A program may use at most 64 MiB of HBM per device.

v0:
```python
import jax
import jax.numpy as jnp
from jax import lax
from jax.sharding import PartitionSpec as P

NDISP = 2


def signs_over(matrix_order):
    eigen_count = matrix_order // 4
    spin = jnp.arange(matrix_order, dtype=jnp.int32) // eigen_count
    return jnp.where(spin < 2, 1.0, -1.0).astype(jnp.float32)


def contract(left, right, contracted):
    return lax.dot_general(left, right, (contracted, ((), ())), preferred_element_type=jnp.float32)


def sink_columns(cols_real, cols_imag, e_real, e_imag, spin_signs):
    column_count, matrix_order = cols_real.shape
    eigen_count = e_real.shape[0]
    flat_real = cols_real.reshape(column_count * 4, eigen_count)
    flat_imag = cols_imag.reshape(column_count * 4, eigen_count)
    contracted = ((1,), (1,))
    x_real = contract(flat_real, e_real, contracted) - contract(flat_imag, e_imag, contracted)
    x_imag = contract(flat_real, e_imag, contracted) + contract(flat_imag, e_real, contracted)
    x_real = (x_real.reshape(column_count, matrix_order) * spin_signs).astype(jnp.bfloat16)
    x_imag = (x_imag.reshape(column_count, matrix_order) * spin_signs).astype(jnp.bfloat16)
    return (x_real, x_imag)


def pair_loop(xt_real, xt_imag, prop_real, prop_imag, f_real, f_imag, spin_signs):
    matrix_order = prop_real.shape[0]
    eigen_count = matrix_order // 4
    cube_real = prop_real.reshape(4, eigen_count, matrix_order)
    cube_imag = prop_imag.reshape(4, eigen_count, matrix_order)
    contracted = ((1,), (1,))
    y_real = contract(cube_real, f_real, contracted) + contract(cube_imag, f_imag, contracted)
    y_imag = contract(cube_real, f_imag, contracted) - contract(cube_imag, f_real, contracted)
    y_real = (y_real * spin_signs[None, :, None]).astype(jnp.bfloat16)
    y_imag = (y_imag * spin_signs[None, :, None]).astype(jnp.bfloat16)
    left_real = xt_real.reshape(4, eigen_count, matrix_order)
    left_imag = xt_imag.reshape(4, eigen_count, matrix_order)
    joined = ((0, 1), (0, 2))
    m_real = contract(left_real, y_real, joined) - contract(left_imag, y_imag, joined)
    m_imag = contract(left_real, y_imag, joined) + contract(left_imag, y_real, joined)
    return jnp.stack([m_real, m_imag], 0).astype(jnp.bfloat16)


def local(perambulator, batch_columns, sink_operator, sink_elemental, source_elemental):
    source_count = perambulator.shape[0]
    sink_count = perambulator.shape[1]
    capacity = perambulator.shape[2]
    matrix_order = perambulator.shape[4]
    devices = lax.axis_size("ta")
    pair_dev = source_count * sink_count // devices
    rank_here = lax.axis_index("ta")
    spin_signs = signs_over(matrix_order)
    counts = lax.all_gather(batch_columns, "ta", axis=0, tiled=True)
    starts = jnp.cumsum(counts) - counts
    operators = sink_operator[0] * NDISP + sink_operator[1]
    chosen = sink_elemental[operators, jnp.arange(sink_count)]
    outgoing = perambulator[:, :, None]
    carried_count = 1
    outgoing = outgoing.reshape(devices, pair_dev, carried_count, capacity, 2, matrix_order)
    received = lax.all_to_all(outgoing, "ta", split_axis=0, concat_axis=0, tiled=True)
    column = jnp.arange(matrix_order, dtype=jnp.int32)
    holder = jnp.sum((starts[None, :] <= column[:, None]).astype(jnp.int32), axis=1) - 1
    offset = column - jnp.take(starts, holder)
    columns = received[holder, :, :, offset]
    pair_index = rank_here * pair_dev + 0
    source = pair_index // sink_count
    sink_time = pair_index % sink_count
    propagator = columns[:, 0, carried_count - 1]
    prop_real = propagator[:, 0]
    prop_imag = propagator[:, 1]
    element = lax.dynamic_index_in_dim(chosen, sink_time, 0, keepdims=False)
    xt_real, xt_imag = sink_columns(prop_real, prop_imag, element[0], element[1], spin_signs)
    source_table = lax.dynamic_index_in_dim(source_elemental, source, 0, keepdims=False)
    results = [
        pair_loop(
            xt_real, xt_imag, prop_real, prop_imag, source_table[0], source_table[1], spin_signs
        )
    ]
    return jnp.stack(results, 0)


def solution(mesh):
    placed = (
        P("grp", None, "ta", None, None),
        P(("grp", "ta")),
        P(),
        P("grp", None, None, None, None),
        P("grp", None, None, None),
    )
    return jax.shard_map(
        local,
        mesh=mesh,
        in_specs=placed,
        out_specs=P(("grp", "ta"), None, None, None),
        check_vma=False,
    )
```

profile of v0, /device:TPU:0, one launch (start us, length us, event | category | flops | bytes accessed | tf_op | source)
XLA Modules:
  0.0 94.1 jit_solution(8770418894585019394)
XLA Ops:
  0.0 7.5 %all-to-all-start = ((bf16[16,1,1,48,2,512]{5,4,3,2,1,0:T(2,128)(2,1)}), bf16[16,1,1,48,2,512]{5,4,3,2,1,0:T(2,128)(2,1)S(1)}, u32[]{:S(2)}, u32[]{:S(2)}) async-start(bf16[16,1,1,48,2,512]{5,4,3,2,1,0:T(2,128)(2,1)} %bitcast.97), calls=%async_computation | async-start | bytes 3145728 | tf_op jit(solution)/shard_map/all_to_all | solution.py:66
  8.2 0.6 dynamic-slice
  8.8 0.8 dynamic-update-slice
  9.5 36.0 %all-reduce = s32[16]{0:T(128)S(1)} all-reduce(s32[16]{0:T(128)S(1)} %dynamic-update-slice), channel_id=1, replica_groups=mesh['grp'=2,'ta'=16] {'ta'}, use_global_device_ids=true, to_apply=%add | all-reduce | flops 16 | bytes 128
  45.8 3.8 %gather_fusion.1 = bf16[16,2,128,128]{3,2,1,0:T(8,128)(2,1)} fusion(bf16[4,16,2,128,128]{4,3,2,1,0:T(8,128)(2,1)} %param.8, s32[16]{0:T(128)S(1)} %fusion.34), kind=kCustom, calls=%fused_computation.1 | custom fusion | bytes 2097280 | tf_op jit(solution)/shard_map/gather | solution.py:62
  49.6 0.7 fusion.39
  50.4 4.4 %compare_select_fusion.2 = (s32[512,1]{0,1:T(1,128)S(1)}, s32[512,1]{0,1:T(1,128)S(1)}) fusion(s32[]{:T(128)} %bitcast.15, s32[]{:T(128)} %bitcast.16, s32[]{:T(128)} %bitcast.17, s32[]{:T(128)} %bitcast.18, s32[]{:T(128)} %bitcast.19, s32[]{:T(128)} %bitcast.21, s32[]{:T(128)} %bitcast.20, s32[512,1]{0,1:T(1,128)S(1)} %bitcast.100, s32[512,1]{0,1:T(1,128)S(1)} %bitcast.99), kind=kLoop, calls=%fused_computation.50 | loop fusion | flops 7168 | bytes 8220 | tf_op jit(solution)/shard_map/jit(_take)/gather | solution.py:69
  55.0 5.5 %select_select_fusion = s32[512]{0:T(512)S(1)} fusion(pred[512]{0:T(512)(128)(4,1)S(1)} %get-tuple-element.14, pred[512]{0:T(512)(128)(4,1)S(1)} %get-tuple-element.13, pred[512]{0:T(512)(128)(4,1)S(1)} %get-tuple-element.15, pred[512]{0:T(512)(128)(4,1)S(1)} %get-tuple-element.12, pred[512]{0:T(512)(128)(4,1)S(1)} %get-tuple-element.11, ...), kind=kLoop, calls=%fused_computation.69 | loop fusion | flops 4608 | bytes 8740 | tf_op jit(solution)/shard_map/jit(_take)/gather | solution.py:69
  60.5 3.7 %gather_fusion = bf16[512,2,512]{2,1,0:T(2,128)(2,1)S(1)} fusion(bf16[16,48,2,512]{3,2,1,0:T(2,128)(2,1)S(1)} %bitcast.96, s32[512]{0:T(512)S(1)} %bitcast.91), kind=kCustom, calls=%fused_computation | custom fusion | bytes 2101248 | tf_op jit(solution)/shard_map/gather | solution.py:70
  64.2 7.4 %slice_reduce_fusion = (bf16[512,512]{1,0:T(8,128)(2,1)S(1)}, bf16[512,512]{1,0:T(8,128)(2,1)}, bf16[512,1,512]{2,1,0:T(2,128)(2,1)S(1)}, bf16[512,1,512]{2,1,0:T(2,128)(2,1)S(1)}) fusion(bf16[512,2,512]{2,1,0:T(2,128)(2,1)S(1)} %gather_fusion), kind=kLoop, calls=%fused_computation.82 | loop fusion | bytes 3145728 | tf_op jit(solution)/shard_map/slice | solution.py:76
  71.7 0.7 copy-done.1
  72.4 1.3 %fusion.13 = f32[4,512,128]{2,1,0:T(8,128)} fusion(bf16[4,128,512]{2,1,0:T(8,128)(2,1)S(1)} %bitcast.94, bf16[1,2,128,128]{3,2,1,0:T(8,128)(2,1)S(1)} %copy-done.1), kind=kOutput, calls=%fused_computation.28 | convolution fusion | flops 67108864 | bytes 1605632 | tf_op jit(solution)/shard_map/dot_general | solution.py:16
  73.8 0.3 fusion.11
  74.1 0.3 reshape_squeeze.13
  74.4 1.4 %reshape_squeeze.12 = bf16[2048,128]{1,0:T(8,128)(2,1)S(1)} reshape(bf16[512,512]{1,0:T(8,128)(2,1)} %get-tuple-element.6) | data formatting | bytes 1048576 | tf_op jit(solution)/shard_map/reshape;squeeze | solution.py:22
  75.8 0.1 copy.42
  75.9 1.1 %copy-done = f32[4,512,128]{2,1,0:T(8,128)S(1)} copy-done((f32[4,512,128]{2,1,0:T(8,128)S(1)}, f32[4,512,128]{2,1,0:T(8,128)}, u32[]{:S(2)}) %copy-start) | copy-done | bytes 1048600
  77.0 0.4 fusion.5
  77.4 0.4 fusion.4
  77.8 2.1 %fusion.20 = f32[2048,128]{1,0:T(8,128)} fusion(bf16[2048,128]{1,0:T(8,128)(2,1)S(1)} %reshape_squeeze.12, bf16[16,2,128,128]{3,2,1,0:T(8,128)(2,1)} %gather_fusion.1, s32[]{:T(128)S(6)} %select_n.107), kind=kOutput, calls=%fused_computation.37 | convolution fusion | flops 67108864 | bytes 1605636 | tf_op jit(solution)/shard_map/dot_general | solution.py:16
  79.8 1.1 %fusion.21 = f32[2048,128]{1,0:T(8,128)S(1)} fusion(bf16[2048,128]{1,0:T(8,128)(2,1)S(1)} %reshape_squeeze.12, bf16[16,2,128,128]{3,2,1,0:T(8,128)(2,1)} %gather_fusion.1, s32[]{:T(128)S(6)} %select_n.107, s32[]{:T(128)S(6)} %add.139), kind=kOutput, calls=%fused_computation.38 | convolution fusion | flops 67108864 | bytes 1605640 | tf_op jit(solution)/shard_map/dot_general | solution.py:16
  80.9 1.1 %convolution_add_fusion = f32[2048,128]{1,0:T(8,128)S(1)} fusion(f32[2048,128]{1,0:T(8,128)S(1)} %fusion.21, bf16[2048,128]{1,0:T(8,128)(2,1)S(1)} %reshape_squeeze.13, bf16[16,2,128,128]{3,2,1,0:T(8,128)(2,1)} %gather_fusion.1, s32[]{:T(128)S(6)} %select_n.107), kind=kOutput, calls=%fused_computation.2 | convolution fusion | flops 67371008 | bytes 2654212 | tf_op jit(solution)/shard_map/dot_general | solution.py:16
  81.9 1.2 %reshape.214 = f32[4,128,512]{2,1,0:T(8,128)} reshape(f32[2048,128]{1,0:T(8,128)S(1)} %convolution_add_fusion) | data formatting | bytes 2097152 | tf_op jit(solution)/shard_map/reshape | solution.py:28
  83.1 1.5 %copy.34 = f32[4,128,512]{1,2,0:T(8,128)S(1)} copy(f32[4,128,512]{2,1,0:T(8,128)} %reshape.214) | data formatting | bytes 2097152 | tf_op jit(solution)/shard_map/reshape | solution.py:28
  84.7 2.5 %convolution_subtract_fusion = f32[2048,128]{1,0:T(8,128)} fusion(f32[2048,128]{1,0:T(8,128)} %fusion.20, bf16[2048,128]{1,0:T(8,128)(2,1)S(1)} %reshape_squeeze.13, bf16[16,2,128,128]{3,2,1,0:T(8,128)(2,1)} %gather_fusion.1, s32[]{:T(128)S(6)} %select_n.107, s32[]{:T(128)S(6)} %add.139), kind=kOutput, calls=%fused_computation.3 | convolution fusion | flops 67371008 | bytes 2654216 | tf_op jit(solution)/shard_map/dot_general | solution.py:16
  87.2 2.4 %reshape.213 = f32[4,128,512]{2,1,0:T(8,128)} reshape(f32[2048,128]{1,0:T(8,128)} %convolution_subtract_fusion) | data formatting | bytes 2097152 | tf_op jit(solution)/shard_map/reshape | solution.py:27
  89.6 1.5 %copy.31 = f32[4,128,512]{1,2,0:T(8,128)S(1)} copy(f32[4,128,512]{2,1,0:T(8,128)} %reshape.213) | data formatting | bytes 2097152 | tf_op jit(solution)/shard_map/reshape | solution.py:27
  91.1 0.5 convolution_bitcast_fusion
  91.6 0.5 convolution_bitcast_fusion.2
  92.1 0.5 fusion.9
  92.6 0.5 fusion.8
  93.1 1.1 %pad_maximum_fusion = bf16[1,2,512,512]{3,2,1,0:T(8,128)(2,1)} fusion(bf16[1,1,512,512]{3,2,1,0:T(8,128)(2,1)S(1)} %fusion.9, bf16[1,1,512,512]{3,2,1,0:T(8,128)(2,1)S(1)} %fusion.8), kind=kLoop, calls=%fused_computation.20 | loop fusion | flops 524288 | bytes 2097152 | tf_op jit(solution)/shard_map/stack | solution.py:47
  (19 shorter events, 0.6 us)
Async XLA Ops:
  0.0 8.2 %copy-start.3 = (u32[32]{0:T(128)S(1)}, u32[32]{0:T(128)}, u32[]{:S(2)}) copy-start(u32[32]{0:T(128)} %constant.135) | copy-start | bytes 388
  0.0 45.8 %copy-start.2 = (s32[2,16]{1,0:T(2,128)S(1)}, s32[2,16]{1,0:T(2,128)}, u32[]{:S(2)}) copy-start(s32[2,16]{1,0:T(2,128)} %param.7) | copy-start | bytes 388
  0.0 60.5 %all-to-all-start = ((bf16[16,1,1,48,2,512]{5,4,3,2,1,0:T(2,128)(2,1)}), bf16[16,1,1,48,2,512]{5,4,3,2,1,0:T(2,128)(2,1)S(1)}, u32[]{:S(2)}, u32[]{:S(2)}) async-start(bf16[16,1,1,48,2,512]{5,4,3,2,1,0:T(2,128)(2,1)} %bitcast.97), calls=%async_computation | async-start | bytes 3145728 | tf_op jit(solution)/shard_map/all_to_all | solution.py:66
  71.6 0.8 copy-start.1
  75.8 1.2 %copy-start = (f32[4,512,128]{2,1,0:T(8,128)S(1)}, f32[4,512,128]{2,1,0:T(8,128)}, u32[]{:S(2)}) copy-start(f32[4,512,128]{2,1,0:T(8,128)} %fusion.13) | copy-start | bytes 3145732
where the time goes:
time: 95 us; the launch traced here: 94.1 us
  blocking collectives  36 us (38%)
  local copies, waits for them, and re-layouts  27.4 us (29%)
  other arithmetic  11.4 us (12%)
  matrix products  11 us (12%)
  starting transfers between devices  7.49 us (8%)
    unnamed x1, blocking collectives  36 us
    dot_general x12, matrix products, contract(): lax.dot_general(left, right, (contracted, ((), ())), preferred_element_ty...  11 us
    gather x3, other arithmetic, local(): offset = column - jnp.take(starts, holder)  10 us
    all_to_all x1, starting transfers between devices, local(): lax.all_to_all(outgoing, 'ta', split_axis=0, concat_axis=0, tiled=True)  7.49 us
    slice x1, local copies, waits for them, and re-layouts, local(): prop_imag = propagator[:, 1]  7.36 us
    reshape x2, local copies, waits for them, and re-layouts, sink_columns(): x_real.reshape(column_count, matrix_order) * spin_signs  3.9 us
    gather x1, local copies, waits for them, and re-layouts, local(): chosen = sink_elemental[operators, jnp.arange(sink_count)]  3.84 us
    gather x1, local copies, waits for them, and re-layouts, local(): columns = received[holder, :, :, offset]  3.74 us
  transfers between devices with their start and end apart: 1, of which 0 were waited for; matrix products, arithmetic and copies ran while one was open for 17% of the time, Pallas kernels for 0%

commit v1 on v0

v1 whole, which is shorter than its diff:
```python
import functools

import jax
import jax.numpy as jnp
from jax import lax
from jax.experimental import pallas as pl
from jax.experimental.pallas import tpu as pltpu
from jax.sharding import PartitionSpec as P

NDISP = 2
MESH = pl.DeviceIdType.MESH


def product(left, right, contracted=((1,), (0,))):
    return lax.dot_general(left, right, (contracted, ((), ())), preferred_element_type=jnp.float32)


def kernel(
    devices, sink_count, capacity, group,
    blocks_ref, count_ref, operator_ref, sink_ref, source_ref, out_ref,
    recv, counts, starts, acc, prop_re, prop_im, x_re, x_im, y_re, y_im, y_neg, elems, table,
    send_sem, recv_sem, count_send, count_recv, local_sem,
):
    me = lax.axis_index("ta")
    rows, order = recv.shape[1], recv.shape[2]
    eigen = order // 4
    sink_time = lax.rem(me, sink_count)
    source = me // sink_count

    own = pltpu.make_async_copy(blocks_ref.at[me], recv.at[me], local_sem.at[0])
    own.start()
    fetch_sink = pltpu.make_async_copy(sink_ref.at[:, sink_time], elems, local_sem.at[1])
    fetch_sink.start()
    fetch_source = pltpu.make_async_copy(source_ref.at[source], table, local_sem.at[2])
    fetch_source.start()

    counts[me] = jnp.full(counts.shape[1:], count_ref[0], jnp.int32)

    def peer(step):
        half = (step + 1) // 2
        return devices // 2 + half * (1 - 2 * lax.rem(step, 2))

    barrier = pltpu.get_barrier_semaphore()

    @pl.loop(1, devices)
    def _(k):
        pl.semaphore_signal(barrier, inc=1, device_id={"ta": lax.rem(me + k, devices)}, device_id_type=MESH)

    pl.semaphore_wait(barrier, devices - 1)

    def block_copy(target, slot):
        return pltpu.make_async_remote_copy(
            src_ref=blocks_ref.at[target], dst_ref=recv.at[slot],
            send_sem=send_sem.at[target], recv_sem=recv_sem.at[slot],
            device_id={"ta": target}, device_id_type=MESH,
        )

    def count_copy(target, slot):
        return pltpu.make_async_remote_copy(
            src_ref=counts.at[me], dst_ref=counts.at[slot],
            send_sem=count_send.at[target], recv_sem=count_recv.at[slot],
            device_id={"ta": target}, device_id_type=MESH,
        )

    @pl.loop(1, devices)
    def _(k):
        count_copy(lax.rem(me + k, devices), me).start()

    @pl.loop(0, devices - 1)
    def _(step):
        block_copy(lax.rem(me + peer(step), devices), me).start()

    acc[...] = jnp.zeros_like(acc)
    fetch_source.wait()
    fetch_sink.wait()
    own.wait()

    @pl.loop(1, devices)
    def _(k):
        count_copy(me, lax.rem(me + k, devices)).wait_recv()

    def running(d, total):
        starts[d] = total
        return total + counts[d]

    lax.fori_loop(0, devices, running, jnp.zeros(counts.shape[1:], jnp.int32))

    operator = operator_ref[0, sink_time] * NDISP + operator_ref[1, sink_time]
    element = elems[operator]
    e_real, e_imag = element[0], element[1]
    e_full = jnp.concatenate(
        [jnp.concatenate([e_real, -e_imag], 1), jnp.concatenate([e_imag, e_real], 1)], 0
    )
    f_real, f_imag = table[0], table[1]
    f_full = jnp.concatenate(
        [jnp.concatenate([f_real, f_imag], 1), jnp.concatenate([f_imag, -f_real], 1)], 0
    )

    group_count = devices // group
    my_group = me // group
    width = group * rows
    lane = lax.broadcasted_iota(jnp.int32, (8, width), 1)
    lane_batch = lane // rows
    lane_row = lane - lane_batch * rows
    lane_slot = lane_row // 2
    lane_part = lane_row - lane_slot * 2
    tile = 2 * eigen

    @pl.loop(0, group_count)
    def _(step):
        which = lax.rem(my_group + step, group_count)
        first = which * group

        for g in range(group):
            @pl.when(first + g != me)
            def _():
                block_copy(me, first + g).wait_recv()

        held = jnp.zeros((8, width), jnp.int32)
        begin = jnp.zeros((8, width), jnp.int32)
        for g in range(group):
            here = lane_batch == g
            held = jnp.where(here, counts[first + g][0:1, 0:1], held)
            begin = jnp.where(here, starts[first + g][0:1, 0:1], begin)
        goal = jnp.where(lane_slot < held, lane_part * order + begin + lane_slot, -1)[0:1]
        arrived = recv[pl.ds(first, group)].reshape(width, order)
        for m in range(0, 2 * order, tile):
            index = lax.broadcasted_iota(jnp.int32, (tile, width), 0) + m
            picks = jnp.where(index == goal, 1.0, 0.0).astype(jnp.bfloat16)
            acc[m:m + tile] += product(picks, arrived)

    prop_re[...] = acc[0:order].astype(jnp.bfloat16)
    prop_im[...] = acc[order:2 * order].astype(jnp.bfloat16)

    for s in range(4):
        span = slice(s * eigen, (s + 1) * eigen)
        sign = 1.0 if s < 2 else -1.0
        pair = jnp.concatenate([prop_re[:, span], prop_im[:, span]], 1)
        x = product(e_full, pair, ((1,), (1,))) * sign
        x_re[span] = x[:eigen].astype(jnp.bfloat16)
        x_im[span] = x[eigen:].astype(jnp.bfloat16)

    spin = lax.broadcasted_iota(jnp.int32, (1, order), 1) // eigen
    signs = jnp.where(spin < 2, 1.0, -1.0).astype(jnp.float32)
    for t in range(4):
        span = slice(t * eigen, (t + 1) * eigen)
        stacked = jnp.concatenate([prop_re[span], prop_im[span]], 0)
        y = product(f_full, stacked) * signs
        y_re[span] = y[:eigen].astype(jnp.bfloat16)
        y_im[span] = y[eigen:].astype(jnp.bfloat16)
        y_neg[span] = (-y[eigen:]).astype(jnp.bfloat16)

    for m in range(0, order, tile):
        left_re, left_im = x_re[m:m + tile], x_im[m:m + tile]
        out_ref[0, 0, m:m + tile] = (product(left_re, y_re[...]) + product(left_im, y_neg[...])).astype(jnp.bfloat16)
        out_ref[0, 1, m:m + tile] = (product(left_re, y_im[...]) + product(left_im, y_re[...])).astype(jnp.bfloat16)

    @pl.loop(1, devices)
    def _(k):
        target = lax.rem(me + k, devices)
        count_copy(target, me).wait_send()
        block_copy(target, me).wait_send()


def local(perambulator, batch_columns, sink_operator, sink_elemental, source_elemental):
    source_count, sink_count, capacity, _, order = perambulator.shape
    devices = lax.axis_size("ta")
    pairs = source_count * sink_count
    eigen = order // 4
    blocks = perambulator.reshape(pairs, capacity * 2, order)
    extra = -(capacity * 2) % 16
    if extra:
        blocks = jnp.pad(blocks, ((0, 0), (0, extra), (0, 0)))
    rows = capacity * 2 + extra
    group = max(g for g in range(1, devices + 1) if devices % g == 0 and (g == 1 or g * rows <= 256))
    operators = sink_elemental.shape[0]
    vmem = pl.BlockSpec(memory_space=pltpu.VMEM)
    smem = pl.BlockSpec(memory_space=pltpu.SMEM)
    hbm = pl.BlockSpec(memory_space=pl.ANY)
    square = pltpu.VMEM((order, order), jnp.bfloat16)
    return pl.pallas_call(
        functools.partial(kernel, devices, sink_count, capacity, group),
        out_shape=jax.ShapeDtypeStruct((1, 2, order, order), jnp.bfloat16),
        in_specs=[hbm, smem, smem, hbm, hbm],
        out_specs=vmem,
        scratch_shapes=[
            pltpu.VMEM((devices, rows, order), jnp.bfloat16),
            pltpu.VMEM((devices, 8, 128), jnp.int32),
            pltpu.VMEM((devices, 8, 128), jnp.int32),
            pltpu.VMEM((2 * order, order), jnp.float32),
            square, square, square, square, square, square, square,
            pltpu.VMEM((operators, 2, eigen, eigen), jnp.bfloat16),
            pltpu.VMEM((2, eigen, eigen), jnp.bfloat16),
            pltpu.SemaphoreType.DMA((devices,)),
            pltpu.SemaphoreType.DMA((devices,)),
            pltpu.SemaphoreType.DMA((devices,)),
            pltpu.SemaphoreType.DMA((devices,)),
            pltpu.SemaphoreType.DMA((3,)),
        ],
        compiler_params=pltpu.CompilerParams(
            collective_id=0, has_side_effects=True, vmem_limit_bytes=40 * 1024 * 1024
        ),
    )(blocks, batch_columns, sink_operator, sink_elemental, source_elemental)


def solution(mesh):
    placed = (
        P("grp", None, "ta", None, None),
        P(("grp", "ta")),
        P(),
        P("grp", None, None, None, None),
        P("grp", None, None, None),
    )
    return jax.shard_map(
        local,
        mesh=mesh,
        in_specs=placed,
        out_specs=P(("grp", "ta"), None, None, None),
        check_vma=False,
    )
```

time: 95 us -> 54.2 us (0.57)
  the two profiles are of different devices: /device:TPU:0 before, /device:TPU:11 now
where the time goes in v1:
time: 54.2 us; the launch traced here: 53.9 us
  Pallas kernels  47.5 us (88%)
  local copies, waits for them, and re-layouts  5.69 us (10%)
  between operations  0.71 us (1%)
    pallas_call x1, Pallas kernels, local(): pl.pallas_call(functools.partial(kernel, devices, sink_count, capacity, g...  47.5 us
    unnamed x7, local copies, waits for them, and re-layouts  3.16 us
    reshape x1, local copies, waits for them, and re-layouts, local(): blocks = perambulator.reshape(pairs, capacity * 2, order)  2.53 us

profile of v1, /device:TPU:11, one launch (start us, length us, event | category | flops | bytes accessed | tf_op | source)
XLA Modules:
  0.0 53.9 jit_solution(14776030536975458688)
XLA Ops:
  0.7 0.0 copy-start.1
  0.7 0.0 copy-start.2
  0.7 2.5 %reshape.3.blocks_ref = bf16[16,96,512]{2,1,0:T(8,128)(2,1)S(1)} reshape(bf16[1,16,48,2,512]{4,3,2,1,0:T(2,128)(2,1)} %param.5) | data formatting | bytes 3145728 | tf_op jit(solution)/shard_map/reshape | solution.py:170
  3.2 0.0 copy-done.1
  3.2 0.0 copy-done.2
  3.2 0.0 copy-start
  3.2 2.2 %copy-done = bf16[4,16,2,128,128]{4,3,2,1,0:T(8,128)(2,1)S(1)} copy-done((bf16[4,16,2,128,128]{4,3,2,1,0:T(8,128)(2,1)S(1)}, bf16[4,16,2,128,128]{4,3,2,1,0:T(8,128)(2,1)}, u32[]{:S(2)}) %copy-start) | copy-done | bytes 4194328
  5.4 47.5 %shard_map.55 = bf16[1,2,512,512]{3,2,1,0:T(8,128)(2,1)S(1)} custom-call(bf16[16,96,512]{2,1,0:T(8,128)(2,1)S(1)} %reshape.3.blocks_ref, s32[1]{0:T(128)S(6)} %copy.7.count_ref, s32[2,16]{1,0:T(2,128)S(1)} %copy-done.2, bf16[4,16,2,128,128]{4,3,2,1,0:T(8,128)(2,1)S(1)} %copy-done, bf16[1,2,128,128]{3,2,1,0:T(8,128)(2,1)S(1)} %copy-done.1), custom_call_target="tpu_custom_call" | custom-call | tf_op jit(solution)/shard_map/pallas_call | solution.py:181
  53.0 1.0 %copy.8 = bf16[1,2,512,512]{3,2,1,0:T(8,128)(2,1)} copy(bf16[1,2,512,512]{3,2,1,0:T(8,128)(2,1)S(1)} %shard_map.55) | data formatting | bytes 2097152
Async XLA Ops:
  0.7 2.6 %copy-start.1 = (bf16[1,2,128,128]{3,2,1,0:T(8,128)(2,1)S(1)}, bf16[1,2,128,128]{3,2,1,0:T(8,128)(2,1)}, u32[]{:S(2)}) copy-start(bf16[1,2,128,128]{3,2,1,0:T(8,128)(2,1)} %source_ref.1) | copy-start | bytes 196612
  0.7 2.6 %copy-start.2 = (s32[2,16]{1,0:T(2,128)S(1)}, s32[2,16]{1,0:T(2,128)}, u32[]{:S(2)}) copy-start(s32[2,16]{1,0:T(2,128)} %operator_ref.1) | copy-start | bytes 388
  3.2 2.2 %copy-start = (bf16[4,16,2,128,128]{4,3,2,1,0:T(8,128)(2,1)S(1)}, bf16[4,16,2,128,128]{4,3,2,1,0:T(8,128)(2,1)}, u32[]{:S(2)}) copy-start(bf16[4,16,2,128,128]{4,3,2,1,0:T(8,128)(2,1)} %sink_ref.1) | copy-start | bytes 12582916

commit v2 on v1

--- a/solution.py
+++ b/solution.py
@@ -22,7 +22,7 @@
     send_sem, recv_sem, count_send, count_recv, local_sem,
 ):
     me = lax.axis_index("ta")
-    rows, order = recv.shape[1], recv.shape[2]
+    rows, order = 2 * recv.shape[1], recv.shape[3]
     eigen = order // 4
     sink_time = lax.rem(me, sink_count)
     source = me // sink_count
@@ -37,8 +37,7 @@
     counts[me] = jnp.full(counts.shape[1:], count_ref[0], jnp.int32)
 
     def peer(step):
-        half = (step + 1) // 2
-        return devices // 2 + half * (1 - 2 * lax.rem(step, 2))
+        return step + 1
 
     barrier = pltpu.get_barrier_semaphore()
 
@@ -167,10 +166,10 @@
     devices = lax.axis_size("ta")
     pairs = source_count * sink_count
     eigen = order // 4
-    blocks = perambulator.reshape(pairs, capacity * 2, order)
+    blocks = perambulator.reshape(pairs, capacity, 2, order)
     extra = -(capacity * 2) % 16
     if extra:
-        blocks = jnp.pad(blocks, ((0, 0), (0, extra), (0, 0)))
+        blocks = jnp.pad(blocks, ((0, 0), (0, extra // 2), (0, 0), (0, 0)))
     rows = capacity * 2 + extra
     group = max(g for g in range(1, devices + 1) if devices % g == 0 and (g == 1 or g * rows <= 256))
     operators = sink_elemental.shape[0]
@@ -184,7 +183,7 @@
         in_specs=[hbm, smem, smem, hbm, hbm],
         out_specs=vmem,
         scratch_shapes=[
-            pltpu.VMEM((devices, rows, order), jnp.bfloat16),
+            pltpu.VMEM((devices, rows // 2, 2, order), jnp.bfloat16),
             pltpu.VMEM((devices, 8, 128), jnp.int32),
             pltpu.VMEM((devices, 8, 128), jnp.int32),
             pltpu.VMEM((2 * order, order), jnp.float32),
@@ -198,7 +197,7 @@
             pltpu.SemaphoreType.DMA((3,)),
         ],
         compiler_params=pltpu.CompilerParams(
-            collective_id=0, has_side_effects=True, vmem_limit_bytes=40 * 1024 * 1024
+            collective_id=0, has_side_effects=True, vmem_limit_bytes=60 * 1024 * 1024
         ),
     )(blocks, batch_columns, sink_operator, sink_elemental, source_elemental)
 

time: 54.2 us -> 51 us (0.941)
  local copies, waits for them, and re-layouts: 5.69 us -> 2.26 us
    reshape x1 -> x0, local copies, waits for them, and re-layouts: 2.53 us -> none  [local(): blocks = perambulator.reshape(pairs, capacity * 2, order)]
    unnamed x7 -> x1, local copies, waits for them, and re-layouts: 3.16 us -> 2.26 us
where the time goes in v2:
time: 51 us; the launch traced here: 50.8 us
  Pallas kernels  47.9 us (94%)
  local copies, waits for them, and re-layouts  2.26 us (4%)
  between operations  0.66 us (1%)
    pallas_call x1, Pallas kernels, local(): pl.pallas_call(functools.partial(kernel, devices, sink_count, capacity, g...  47.9 us
    unnamed x1, local copies, waits for them, and re-layouts  2.26 us

profile of v2, /device:TPU:11, one launch (start us, length us, event | category | flops | bytes accessed | tf_op | source)
XLA Modules:
  0.0 50.8 jit_solution(13121879213169041341)
XLA Ops:
  0.7 47.9 %shard_map.55 = bf16[1,2,512,512]{3,2,1,0:T(8,128)(2,1)} custom-call(bf16[16,48,2,512]{3,2,1,0:T(2,128)(2,1)} %bitcast.1, s32[1]{0:T(128)S(6)} %copy.7.count_ref, s32[2,16]{1,0:T(2,128)} %operator_ref.1, bf16[4,16,2,128,128]{4,3,2,1,0:T(8,128)(2,1)} %sink_ref.1, bf16[1,2,128,128]{3,2,1,0:T(8,128)(2,1)} %source_ref.1), custom_call_target="tpu_custom_call" | custom-call | tf_op jit(solution)/shard_map/pallas_call | solution.py:180
  48.6 2.3 %copy.8 = bf16[1,2,512,512]{3,2,1,0:T(8,128)(2,1)} copy(bf16[1,2,512,512]{3,2,1,0:T(8,128)(2,1)} %shard_map.55) | data formatting | bytes 2097152
